TPU v7x, 32 devices: a whole 2x2x4 slice. The times are simulated.
32 devices in a mesh: parts: 2 (over y), dp: 8 (over z, x), tensor: 2 (over core).
Axes of the slice: x: 2, y: 2, z: 4, core: 2. Of those that a mesh axis runs over, the one named last changes fastest.
Arguments:
- activations: bfloat16 [2, 8192, 25600], P(None, ('parts', 'dp'), 'tensor'), parts along dimension 1, may hold values from -6 to 6
- out_grads: bfloat16 [2, 8192, 5120], P(None, ('parts', 'dp'), 'tensor'), parts along dimension 1, may hold values from -6 to 6
- proj_in: bfloat16 [25600, 64], P('tensor'), may hold values from -0.0390625 to 0.0390625
- proj_out: bfloat16 [5120, 64], P('tensor'), may hold values from -0.078125 to 0.078125
- token_ids: int32 [32, 256], P(('parts', 'dp')), parts along dimension 0, may hold values from 0 to 151643, as said below
- queries: bfloat16 [2, 2048, 4096], P(None, 'tensor', 'dp'), may hold values from -6 to 6
- query_docs: int32 [4096, 8], P(('parts', 'tensor')), parts along dimension 0, may hold values from 0 to 15, all different within a row
Outputs:
- scores: float32 [32, 2048], P(('parts', 'dp'), 'tensor'), parts along dimension 0
- listed: float32 [4096], P(('parts', 'tensor')), parts along dimension 0
There are 2 independent parts, one for each index of `parts`. A program takes and returns all parts, laid end to end along the dimension named above; an argument that names none is the same for every part. Nothing has to cross between parts.
Inputs may be any that keep to these rules, and one draw needn't show every extreme that they name: `token_ids`: each document is a run of real token ids below 151643 followed by padding id 151643 up to its end; it has at least 64 real tokens, and some document is padded. `query_docs`: each query lists 8 different documents.
All inputs are finite; a program needn't handle non-finite values.
Results may differ from a plain program's by a relative error of at most 0.0029.
Values may be sent and summed in bfloat16 or wider, within the bound.
No kernel may reach another device: no remote copies, remote signals or barrier semaphores. Data moves between devices by JAX's collectives and lax.ppermute only.
A program may use at most 128 MiB of HBM per device.

v0:
```python
import functools

import jax
import jax.numpy as jnp
from jax import lax
from jax.experimental import pallas as pl
from jax.experimental.pallas import tpu as pltpu
from jax.sharding import PartitionSpec as P

PAD = 151643
BLOCK = 32
STEP = 2
VMEM = pl.BlockSpec(memory_space=pltpu.VMEM)
HBM = pl.BlockSpec(memory_space=pltpu.HBM)
LAST = (((1,), (1,)), ((), ()))


def project_kernel(
    doc_len, acts_ref, outs_ref, in_ref, out_ref, ids_ref, queries_ref, listing_ref,
    mine_ref, theirs_ref, near_queries_ref, near_listing_ref, wide, factor, found_both, ids, wide_sems, sems
):
    checkpoints, tokens, in_width = acts_ref.shape
    rank, out_width = out_ref.shape
    docs = tokens // doc_len
    blocks = doc_len // BLOCK
    keeps = lax.axis_index("tensor")
    in_cut, out_cut = pl.ds(0, in_width), pl.ds(in_width, out_width)

    def place(i, first):
        doc = jnp.where(i < first, 0, 1)
        return doc, i - doc * first

    def block_copies(i, doc, block):
        slot = i + 1
        rows = pl.ds(pl.multiple_of(doc * doc_len + block * BLOCK, BLOCK), BLOCK)
        return [
            pltpu.make_async_copy(source.at[:, rows], wide.at[slot, :, :, cut], wide_sems.at[slot])
            for source, cut in ((acts_ref, in_cut), (outs_ref, out_cut))
        ]

    def start(copies):
        for copy in copies:
            copy.start()

    def wait(copies):
        for copy in copies:
            copy.wait()

    ids_copy = pltpu.make_async_copy(ids_ref, ids, sems.at[0])
    factor_copies = [
        pltpu.make_async_copy(in_ref, factor.at[pl.ds(0, rank), in_cut], sems.at[1]),
        pltpu.make_async_copy(out_ref, factor.at[pl.ds(rank, rank), out_cut], sems.at[2]),
    ]
    late_copies = [
        pltpu.make_async_copy(queries_ref, near_queries_ref, sems.at[3]),
        pltpu.make_async_copy(listing_ref, near_listing_ref, sems.at[4]),
    ]

    ids_copy.start()
    start(factor_copies)
    for block in range(STEP):
        start(block_copies(block, 0, block))
    factor[:rank, in_width:] = jnp.zeros((rank, out_width), factor.dtype)
    factor[rank:, :in_width] = jnp.zeros((rank, in_width), factor.dtype)
    ids_copy.wait()
    first, second = (
        sum((ids[doc, block * BLOCK] != PAD).astype(jnp.int32) for block in range(blocks)) for doc in range(docs)
    )

    total = first + second

    def start_block(i, carry):
        start(block_copies(i, *place(i, first)))
        return carry

    lax.fori_loop(STEP, total, start_block, 0)
    start(late_copies)

    found_both[...] = jnp.zeros_like(found_both)

    def put(i, found):
        doc, block = place(i, first)
        line = jnp.concatenate([found[c * BLOCK : (c + 1) * BLOCK] for c in range(checkpoints)], axis=1)
        at = pl.ds(pl.multiple_of(block * BLOCK, BLOCK), BLOCK)

        found_both[jnp.where(doc == keeps, 0, 1), at] = line

    def wait_block(i):
        slot = wide.at[i + 1]
        pltpu.make_async_copy(slot, slot, wide_sems.at[i + 1]).wait()

    odd = lax.rem(total, STEP)

    def step(j, carry):
        i = j * STEP - odd
        pl.when(i >= 0)(lambda: wait_block(i))
        wait_block(i + 1)
        rows = checkpoints * BLOCK
        found = lax.dot_general(
            wide[pl.ds(i + 1, STEP)].reshape(STEP * rows, in_width + out_width),
            factor[...],
            LAST,
            preferred_element_type=jnp.float32,
        )
        pl.when(i >= 0)(lambda: put(i, found[:rows]))
        put(i + 1, found[rows:])
        return carry

    wait(factor_copies)
    lax.fori_loop(0, (total + odd) // STEP, step, 0)
    mine_ref[...] = found_both[0]
    theirs_ref[...] = found_both[1]
    wait(late_copies)


def grad_kernel(dp, tensor, checkpoints, ids_ref, mine_ref, other_ref, sent_ref):
    doc_len, lanes = mine_ref.shape
    pair = lanes // checkpoints
    rank = pair // 2
    rows = rank // dp
    ids = ids_ref[pl.ds(lax.axis_index("tensor"), 1), :]
    keep = jnp.where(ids != PAD, doc_len**-0.5, 0.0)
    sides = mine_ref[...] + other_ref[...]
    in_side, out_side = (
        jnp.concatenate([sides[:, c * pair + at : c * pair + at + rank] for c in range(checkpoints)], axis=1)
        for at in (0, rank)
    )
    sums = jnp.dot(
        out_side.T * keep, in_side, precision=lax.Precision.HIGHEST, preferred_element_type=jnp.float32
    )
    grads = jnp.concatenate(
        [sums[c * rank : (c + 1) * rank, c * rank : (c + 1) * rank] for c in range(checkpoints)], axis=1
    )
    for j in range(dp):
        for k in range(tensor):
            sent_ref[j * tensor + k] = grads[j * rows : (j + 1) * rows].astype(sent_ref.dtype)


def score_kernel(dp, checkpoints, terms_ref, queries_ref, listed_ref, sent_ref):
    all_docs, rows, lanes = terms_ref.shape
    rank = lanes // checkpoints
    docs = all_docs // dp
    terms = terms_ref[...].astype(jnp.float32)
    parts = [terms[:, r, :].astype(jnp.bfloat16) for r in range(rows)]
    part = None
    for c in range(checkpoints):
        grads = jnp.concatenate([p[:, c * rank : (c + 1) * rank] for p in parts], axis=1)
        term = lax.dot_general(grads, queries_ref[c], LAST, preferred_element_type=jnp.float32)
        part = term if part is None else part + term
    part = part * (1.0 / rank)
    places = listed_ref.shape[0]
    every = lax.broadcasted_iota(jnp.int32, part.shape, 0)
    weight = jnp.zeros(part.shape, jnp.float32)
    for k in range(places):
        weight += jnp.where(listed_ref[k : k + 1, :] == every, 1.0 / places, 0.0)
    own = jnp.sum(weight * part, axis=0, keepdims=True)
    lines = part.shape[1] // 128
    for line in range(lines):
        at = slice(line * 128, (line + 1) * 128)
        for j in range(dp):
            for doc in range(docs):
                n = j * docs + doc
                sent_ref[j, pl.ds(doc * lines + line, 1), :] = part[n : n + 1, at]
            sent_ref[j, pl.ds(docs * lines + line, 1), :] = own[:, at]


def total_kernel(parts_ref, scores_ref, listed_ref):
    docs, columns = scores_ref.shape
    lines = columns // 128
    total = parts_ref[0]
    for i in range(1, parts_ref.shape[0]):
        total += parts_ref[i]
    for line in range(lines):
        at = slice(line * 128, (line + 1) * 128)
        for doc in range(docs):
            n = doc * lines + line
            scores_ref[doc : doc + 1, at] = total[n : n + 1]
        n = docs * lines + line
        listed_ref[:, at] = total[n : n + 1]


def pair_body(dp, tensor, activations, out_grads, proj_in, proj_out, token_ids, queries, query_docs):
    checkpoints, tokens, _ = activations.shape
    rank = proj_in.shape[1]
    docs, doc_len = token_ids.shape
    rows = rank // dp
    own_queries = queries.shape[1]
    lanes = checkpoints * rank
    wide = activations.size + out_grads.size
    width = activations.shape[2] + out_grads.shape[2]
    f32 = jnp.float32

    near = (activations, out_grads, proj_in.T, proj_out.T, token_ids, queries, query_docs.T)
    mine, theirs, near_queries, near_listing = pl.pallas_call(
        functools.partial(project_kernel, doc_len),
        in_specs=[HBM] * 7,
        out_specs=[VMEM] * 4,
        out_shape=[
            pltpu.VMEM((doc_len, 2 * lanes), f32),
            pltpu.VMEM((doc_len, 2 * lanes), f32),
            pltpu.VMEM(queries.shape, queries.dtype),
            pltpu.VMEM(query_docs.shape[::-1], query_docs.dtype),
        ],
        scratch_shapes=[
            pltpu.VMEM((tokens // BLOCK + 1, checkpoints, BLOCK, width), activations.dtype),
            pltpu.VMEM((2 * rank, width), proj_in.dtype),
            pltpu.VMEM((docs, doc_len, 2 * lanes), f32),
            pltpu.SMEM(token_ids.shape, token_ids.dtype),
            pltpu.SemaphoreType.DMA((tokens // BLOCK + 1,)),
            pltpu.SemaphoreType.DMA((5,)),
        ],
        compiler_params=pltpu.CompilerParams(vmem_limit_bytes=46 << 20),
        cost_estimate=pl.CostEstimate(flops=2 * wide * rank, bytes_accessed=2 * wide, transcendentals=0),
        name="project",
    )(*(pltpu.with_memory_space_constraint(x, pltpu.HBM) for x in near))
    other = lax.ppermute(theirs, "tensor", [(0, 1), (1, 0)])
    sent = pl.pallas_call(
        functools.partial(grad_kernel, dp, tensor, checkpoints),
        in_specs=[VMEM] * 3,
        out_specs=VMEM,
        out_shape=jax.ShapeDtypeStruct((dp * tensor, rows, lanes), jnp.bfloat16),
        compiler_params=pltpu.CompilerParams(vmem_limit_bytes=4 << 20),
        name="doc_grads",
    )(token_ids, mine, other)
    terms = lax.all_to_all(sent, ("dp", "tensor"), 0, 0, tiled=True)
    parts = pl.pallas_call(
        functools.partial(score_kernel, dp, checkpoints),
        in_specs=[VMEM] * 3,
        out_specs=VMEM,
        out_shape=jax.ShapeDtypeStruct((dp, (docs + 1) * own_queries // 128, 128), f32),
        compiler_params=pltpu.CompilerParams(vmem_limit_bytes=8 << 20),
        name="partial_scores",
    )(terms, near_queries, near_listing)
    parts = lax.all_to_all(parts, "dp", 0, 0, tiled=True)
    scores, listed = pl.pallas_call(
        total_kernel,
        in_specs=[VMEM],
        out_specs=[VMEM] * 2,
        out_shape=[jax.ShapeDtypeStruct((docs, own_queries), f32), jax.ShapeDtypeStruct((1, own_queries), f32)],
        compiler_params=pltpu.CompilerParams(vmem_limit_bytes=4 << 20),
        name="totals",
    )(parts)
    return scores, listed.reshape(own_queries)


def sum_over_tensor(part, size):
    if size == 2:
        return part + lax.ppermute(part, "tensor", [(0, 1), (1, 0)])
    return lax.psum(part, "tensor")


def any_body(dp, tensor, activations, out_grads, proj_in, proj_out, token_ids, queries, query_docs):
    checkpoints = activations.shape[0]
    rank = proj_in.shape[1]
    docs, doc_len = token_ids.shape
    rows = rank // dp
    own_queries = queries.shape[1]

    out_part = jnp.einsum("ctd,dr->ctr", out_grads, proj_out, preferred_element_type=jnp.float32)
    out_proj = sum_over_tensor(out_part, tensor)
    in_part = jnp.einsum("ctf,fr->ctr", activations, proj_in, preferred_element_type=jnp.float32)
    keep = (token_ids != PAD).astype(jnp.float32).reshape(1, docs, doc_len, 1)
    out_proj = out_proj.reshape(checkpoints, docs, doc_len, rank) * keep
    in_part = in_part.reshape(checkpoints, docs, doc_len, rank)
    term = jnp.einsum("cntr,cnts->crns", out_proj, in_part, precision=lax.Precision.HIGHEST)
    term = term.reshape(checkpoints, dp, 1, rows, docs * rank).transpose(1, 2, 0, 3, 4)
    term = jnp.broadcast_to(term, (dp, tensor, checkpoints, rows, docs * rank))
    term = term.reshape(dp * tensor, checkpoints, rows, docs * rank)
    terms = lax.all_to_all(term, ("dp", "tensor"), 0, 0, tiled=True)
    grads = terms.reshape(dp, tensor, checkpoints, rows, docs, rank).sum(1) * doc_len ** (-0.5)
    grads = grads.astype(jnp.bfloat16).transpose(1, 0, 3, 2, 4).reshape(checkpoints, dp * docs, rows * rank)

    part = jnp.einsum("cnf,cqf->nq", grads, queries, preferred_element_type=jnp.float32)
    every_doc = jnp.arange(dp * docs, dtype=jnp.int32)
    listing = (query_docs.T[None] == every_doc[:, None, None]).sum(1).astype(jnp.float32)
    listed_part = (listing * part).sum(0)
    sent = jnp.concatenate(
        [
            part.reshape(dp, docs, own_queries),
            jnp.broadcast_to(listed_part, (dp, 1, own_queries)),
        ],
        axis=1,
    )
    total = lax.all_to_all(sent, "dp", 0, 0, tiled=True).sum(0) / rank
    return total[:docs], total[docs] / query_docs.shape[1]


def solution(mesh):
    dp, tensor = mesh.shape["dp"], mesh.shape["tensor"]

    def body(*arrays):
        docs, doc_len = arrays[4].shape
        whole_tiles = all(n % 128 == 0 for n in (arrays[0].shape[2], arrays[1].shape[2], arrays[5].shape[1]))
        paired = tensor == 2 and docs == 2 and doc_len % (STEP * BLOCK) == 0 and whole_tiles
        return (pair_body if paired else any_body)(dp, tensor, *arrays)

    in_specs = (
        P(None, ("parts", "dp"), "tensor"),
        P(None, ("parts", "dp"), "tensor"),
        P("tensor", None),
        P("tensor", None),
        P(("parts", "dp"), None),
        P(None, "tensor", "dp"),
        P(("parts", "tensor"), None),
    )
    out_specs = (P(("parts", "dp"), "tensor"), P(("parts", "tensor")))
    return jax.shard_map(
        body,
        mesh=mesh,
        in_specs=in_specs,
        out_specs=out_specs,
        check_vma=False,
    )
```

profile of v0, /device:TPU:0, one launch (start us, length us, event | category | flops | bytes accessed | tf_op | source)
XLA Modules:
  0.0 39.2 jit_solution(4191109345953329174)
XLA Ops:
  0.6 0.0 copy-start
  0.6 9.0 %project.1 = (f32[256,256]{1,0:T(8,128)S(1)}, f32[256,256]{1,0:T(8,128)S(1)}, bf16[2,1024,512]{2,1,0:T(8,128)(2,1)S(1)}, s32[8,1024]{1,0:T(8,128)S(1)}) custom-call(bf16[2,512,12800]{2,1,0:T(8,128)(2,1)} %acts_ref.1, bf16[2,512,2560]{2,1,0:T(8,128)(2,1)} %outs_ref.1, bf16[64,12800]{1,0:T(8,128)(2,1)} %bitcast.4, bf16[64,2560]{1,0:T(8,128)(2,1)} %bitcast.5, ...), custom_call_target="tpu_custom_call" | custom-call | flops 2013265920 | bytes 31457280 | tf_op jit(solution)/shard_map/project/pallas_call | solution.py:194
  9.6 0.5 %collective-permute-start = (f32[256,256]{1,0:T(8,128)S(1)}, f32[256,256]{1,0:T(8,128)S(1)}, u32[]{:S(2)}, u32[]{:S(2)}) collective-permute-start(f32[256,256]{1,0:T(8,128)S(1)} %get-tuple-element.9), channel_id=1, source_target_pairs={{0,1},{1,0},{2,3},{3,2},{4,5},{5,4},{6,7},{7,6},{8,9},{9,8},{10,11... | collective-permute-start | bytes 786440 | tf_op jit(solution)/shard_map/ppermute | solution.py:216
  10.1 1.2 %collective-permute-done.other_ref = f32[256,256]{1,0:T(8,128)S(1)} collective-permute-done((f32[256,256]{1,0:T(8,128)S(1)}, f32[256,256]{1,0:T(8,128)S(1)}, u32[]{:S(2)}, u32[]{:S(2)}) %collective-permute-start) | collective-permute-done | bytes 262176 | tf_op jit(solution)/shard_map/ppermute | solution.py:216
  11.3 0.0 copy-done
  11.3 0.4 %doc_grads.1 = bf16[16,8,128]{2,1,0:T(8,128)(2,1)S(1)} custom-call(s32[2,256]{1,0:T(2,128)S(1)} %copy-done, f32[256,256]{1,0:T(8,128)S(1)} %get-tuple-element.8.mine_ref, f32[256,256]{1,0:T(8,128)S(1)} %collective-permute-done.other_ref), custom_call_target="tpu_custom_call" | custom-call | tf_op jit(solution)/shard_map/doc_grads/pallas_call | solution.py:217
  11.7 16.7 %all_to_all.10.terms_ref = bf16[16,8,128]{2,1,0:T(8,128)(2,1)S(1)} all-to-all(bf16[16,8,128]{2,1,0:T(8,128)(2,1)S(1)} %doc_grads.1), channel_id=1, replica_groups=mesh['parts'=2,'dp'=8,'tensor'=2] {'dp','tensor'}, dimensions={0} | all-to-all | bytes 65536 | tf_op jit(solution)/shard_map/all_to_all | solution.py:225
  28.4 0.7 %partial_scores.1 = f32[8,24,128]{2,1,0:T(8,128)S(1)} custom-call(bf16[16,8,128]{2,1,0:T(8,128)(2,1)S(1)} %all_to_all.10.terms_ref, bf16[2,1024,512]{2,1,0:T(8,128)(2,1)S(1)} %get-tuple-element.10.queries_ref, s32[8,1024]{1,0:T(8,128)S(1)} %get-tuple-element.11.listed_ref), custom_call_target="tpu_custom_call" | custom-call | tf_op jit(solution)/shard_map/partial_scores/pallas_call | solution.py:226
  29.1 9.5 %all_to_all.11.parts_ref = f32[8,24,128]{2,1,0:T(8,128)S(1)} all-to-all(f32[8,24,128]{2,1,0:T(8,128)S(1)} %partial_scores.1), channel_id=1, replica_groups=mesh['parts'=2,'dp'=8,'tensor'=2] {'dp'}, dimensions={0} | all-to-all | bytes 196608 | tf_op jit(solution)/shard_map/all_to_all | solution.py:234
  38.6 0.6 %totals.1 = (f32[2,1024]{1,0:T(2,128)}, f32[1,1024]{1,0:T(1,128)}) custom-call(f32[8,24,128]{2,1,0:T(8,128)S(1)} %all_to_all.11.parts_ref), custom_call_target="tpu_custom_call" | custom-call | tf_op jit(solution)/shard_map/totals/pallas_call | solution.py:235
Async XLA Ops:
  0.6 10.7 %copy-start = (s32[2,256]{1,0:T(2,128)S(1)}, s32[2,256]{1,0:T(2,128)}, u32[]{:S(2)}) copy-start(s32[2,256]{1,0:T(2,128)} %ids_ref.3) | copy-start | bytes 6148
  9.6 1.7 %collective-permute-start = (f32[256,256]{1,0:T(8,128)S(1)}, f32[256,256]{1,0:T(8,128)S(1)}, u32[]{:S(2)}, u32[]{:S(2)}) collective-permute-start(f32[256,256]{1,0:T(8,128)S(1)} %get-tuple-element.9), channel_id=1, source_target_pairs={{0,1},{1,0},{2,3},{3,2},{4,5},{5,4},{6,7},{7,6},{8,9},{9,8},{10,11... | collective-permute-start | bytes 786440 | tf_op jit(solution)/shard_map/ppermute | solution.py:216
where the time goes:
time: 39.5 us; the launch traced here: 39.2 us
  blocking collectives  26.2 us (66%)
  Pallas kernels  10.7 us (27%)
  waiting for transfers between devices  1.16 us (3%)
  between operations  0.67 us (2%)
  starting transfers between devices  0.53 us (1%)
    all_to_all x1, blocking collectives, pair_body(): terms = lax.all_to_all(sent, ('dp', 'tensor'), 0, 0, tiled=True)  16.7 us
    all_to_all x1, blocking collectives, pair_body(): parts = lax.all_to_all(parts, 'dp', 0, 0, tiled=True)  9.51 us
    pallas_call x1, Pallas kernels, pair_body(): pl.pallas_call(functools.partial(project_kernel, doc_len), in_specs=[HBM]...  8.95 us
    ppermute x1, waiting for transfers between devices, pair_body(): other = lax.ppermute(theirs, 'tensor', [(0, 1), (1, 0)])  1.16 us
  transfers between devices with their start and end apart: 1, of which 1 were waited for; matrix products, arithmetic and copies ran while one was open for 0% of the time, Pallas kernels for 0%

commit v1 on v0

--- a/solution.py
+++ b/solution.py
@@ -30,11 +30,11 @@
         doc = jnp.where(i < first, 0, 1)
         return doc, i - doc * first
 
-    def block_copies(i, doc, block):
+    def block_copies(i, doc, block, sem):
         slot = i + 1
         rows = pl.ds(pl.multiple_of(doc * doc_len + block * BLOCK, BLOCK), BLOCK)
         return [
-            pltpu.make_async_copy(source.at[:, rows], wide.at[slot, :, :, cut], wide_sems.at[slot])
+            pltpu.make_async_copy(source.at[:, rows], wide.at[slot, :, :, cut], wide_sems.at[sem])
             for source, cut in ((acts_ref, in_cut), (outs_ref, out_cut))
         ]
 
@@ -59,7 +59,7 @@
     ids_copy.start()
     start(factor_copies)
     for block in range(STEP):
-        start(block_copies(block, 0, block))
+        start(block_copies(block, 0, block, block))
     factor[:rank, in_width:] = jnp.zeros((rank, out_width), factor.dtype)
     factor[rank:, :in_width] = jnp.zeros((rank, in_width), factor.dtype)
     ids_copy.wait()
@@ -68,9 +68,10 @@
     )
 
     total = first + second
+    odd = lax.rem(total, STEP)
 
     def start_block(i, carry):
-        start(block_copies(i, *place(i, first)))
+        start(block_copies(i, *place(i, first), STEP + (i + odd) // STEP))
         return carry
 
     lax.fori_loop(STEP, total, start_block, 0)
@@ -85,16 +86,19 @@
 
         found_both[jnp.where(doc == keeps, 0, 1), at] = line
 
-    def wait_block(i):
-        slot = wide.at[i + 1]
-        pltpu.make_async_copy(slot, slot, wide_sems.at[i + 1]).wait()
-
-    odd = lax.rem(total, STEP)
+    def wait_slots(i, count, sem):
+        slots = wide.at[pl.ds(i + 1, count)]
+        pltpu.make_async_copy(slots, slots, wide_sems.at[sem]).wait()
 
     def step(j, carry):
         i = j * STEP - odd
-        pl.when(i >= 0)(lambda: wait_block(i))
-        wait_block(i + 1)
+
+        @pl.when(i < STEP)
+        def _():
+            pl.when(i >= 0)(lambda: wait_slots(i, 1, i))
+            wait_slots(i + 1, 1, jnp.where(i + 1 < STEP, i + 1, STEP + j))
+
+        pl.when(i >= STEP)(lambda: wait_slots(i, STEP, STEP + j))
         rows = checkpoints * BLOCK
         found = lax.dot_general(
             wide[pl.ds(i + 1, STEP)].reshape(STEP * rows, in_width + out_width),
@@ -206,7 +210,7 @@
             pltpu.VMEM((2 * rank, width), proj_in.dtype),
             pltpu.VMEM((docs, doc_len, 2 * lanes), f32),
             pltpu.SMEM(token_ids.shape, token_ids.dtype),
-            pltpu.SemaphoreType.DMA((tokens // BLOCK + 1,)),
+            pltpu.SemaphoreType.DMA((STEP + tokens // (STEP * BLOCK),)),
             pltpu.SemaphoreType.DMA((5,)),
         ],
         compiler_params=pltpu.CompilerParams(vmem_limit_bytes=46 << 20),

time: 39.5 us -> 37.4 us (0.947); the launches traced: 39.2 us -> 37.6 us
  blocking collectives: 26.2 us -> 25.2 us
  Pallas kernels: 10.7 us -> 10 us
    all_to_all x1, blocking collectives: 16.7 us -> 15.7 us  [pair_body(): terms = lax.all_to_all(sent, ('dp', 'tensor'), 0, 0, tiled=True)]
    pallas_call x1, Pallas kernels: 8.95 us -> 8.34 us  [pair_body(): pl.pallas_call(functools.partial(project_kernel, doc_len), in_specs=[HBM]...]
where the time goes in v1:
time: 37.4 us; the launch traced here: 37.6 us
  blocking collectives  25.2 us (67%)
  Pallas kernels  10 us (27%)
  waiting for transfers between devices  1.16 us (3%)
  between operations  0.67 us (2%)
  starting transfers between devices  0.52 us (1%)
    all_to_all x1, blocking collectives, pair_body(): terms = lax.all_to_all(sent, ('dp', 'tensor'), 0, 0, tiled=True)  15.7 us
    all_to_all x1, blocking collectives, pair_body(): parts = lax.all_to_all(parts, 'dp', 0, 0, tiled=True)  9.51 us
    pallas_call x1, Pallas kernels, pair_body(): pl.pallas_call(functools.partial(project_kernel, doc_len), in_specs=[HBM]...  8.34 us
    ppermute x1, waiting for transfers between devices, pair_body(): other = lax.ppermute(theirs, 'tensor', [(0, 1), (1, 0)])  1.16 us
  transfers between devices with their start and end apart: 1, of which 1 were waited for; matrix products, arithmetic and copies ran while one was open for 0% of the time, Pallas kernels for 0%

profile of v1, /device:TPU:0, one launch (start us, length us, event | category | flops | bytes accessed | tf_op | source)
XLA Modules:
  0.0 37.6 jit_solution(8106420318587145870)
XLA Ops:
  0.6 0.0 copy-start
  0.6 8.3 %project.1 = (f32[256,256]{1,0:T(8,128)S(1)}, f32[256,256]{1,0:T(8,128)S(1)}, bf16[2,1024,512]{2,1,0:T(8,128)(2,1)S(1)}, s32[8,1024]{1,0:T(8,128)S(1)}) custom-call(bf16[2,512,12800]{2,1,0:T(8,128)(2,1)} %acts_ref.1, bf16[2,512,2560]{2,1,0:T(8,128)(2,1)} %outs_ref.1, bf16[64,12800]{1,0:T(8,128)(2,1)} %bitcast.4, bf16[64,2560]{1,0:T(8,128)(2,1)} %bitcast.5, ...), custom_call_target="tpu_custom_call" | custom-call | flops 2013265920 | bytes 31457280 | tf_op jit(solution)/shard_map/project/pallas_call | solution.py:198
  9.0 0.5 %collective-permute-start = (f32[256,256]{1,0:T(8,128)S(1)}, f32[256,256]{1,0:T(8,128)S(1)}, u32[]{:S(2)}, u32[]{:S(2)}) collective-permute-start(f32[256,256]{1,0:T(8,128)S(1)} %get-tuple-element.9), channel_id=1, source_target_pairs={{0,1},{1,0},{2,3},{3,2},{4,5},{5,4},{6,7},{7,6},{8,9},{9,8},{10,11... | collective-permute-start | bytes 786440 | tf_op jit(solution)/shard_map/ppermute | solution.py:220
  9.5 1.2 %collective-permute-done.other_ref = f32[256,256]{1,0:T(8,128)S(1)} collective-permute-done((f32[256,256]{1,0:T(8,128)S(1)}, f32[256,256]{1,0:T(8,128)S(1)}, u32[]{:S(2)}, u32[]{:S(2)}) %collective-permute-start) | collective-permute-done | bytes 262176 | tf_op jit(solution)/shard_map/ppermute | solution.py:220
  10.7 0.0 copy-done
  10.7 0.4 %doc_grads.1 = bf16[16,8,128]{2,1,0:T(8,128)(2,1)S(1)} custom-call(s32[2,256]{1,0:T(2,128)S(1)} %copy-done, f32[256,256]{1,0:T(8,128)S(1)} %get-tuple-element.8.mine_ref, f32[256,256]{1,0:T(8,128)S(1)} %collective-permute-done.other_ref), custom_call_target="tpu_custom_call" | custom-call | tf_op jit(solution)/shard_map/doc_grads/pallas_call | solution.py:221
  11.1 15.7 %all_to_all.10.terms_ref = bf16[16,8,128]{2,1,0:T(8,128)(2,1)S(1)} all-to-all(bf16[16,8,128]{2,1,0:T(8,128)(2,1)S(1)} %doc_grads.1), channel_id=1, replica_groups=mesh['parts'=2,'dp'=8,'tensor'=2] {'dp','tensor'}, dimensions={0} | all-to-all | bytes 65536 | tf_op jit(solution)/shard_map/all_to_all | solution.py:229
  26.8 0.7 %partial_scores.1 = f32[8,24,128]{2,1,0:T(8,128)S(1)} custom-call(bf16[16,8,128]{2,1,0:T(8,128)(2,1)S(1)} %all_to_all.10.terms_ref, bf16[2,1024,512]{2,1,0:T(8,128)(2,1)S(1)} %get-tuple-element.10.queries_ref, s32[8,1024]{1,0:T(8,128)S(1)} %get-tuple-element.11.listed_ref), custom_call_target="tpu_custom_call" | custom-call | tf_op jit(solution)/shard_map/partial_scores/pallas_call | solution.py:230
  27.5 9.5 %all_to_all.11.parts_ref = f32[8,24,128]{2,1,0:T(8,128)S(1)} all-to-all(f32[8,24,128]{2,1,0:T(8,128)S(1)} %partial_scores.1), channel_id=1, replica_groups=mesh['parts'=2,'dp'=8,'tensor'=2] {'dp'}, dimensions={0} | all-to-all | bytes 196608 | tf_op jit(solution)/shard_map/all_to_all | solution.py:238
  37.0 0.6 %totals.1 = (f32[2,1024]{1,0:T(2,128)}, f32[1,1024]{1,0:T(1,128)}) custom-call(f32[8,24,128]{2,1,0:T(8,128)S(1)} %all_to_all.11.parts_ref), custom_call_target="tpu_custom_call" | custom-call | tf_op jit(solution)/shard_map/totals/pallas_call | solution.py:239
Async XLA Ops:
  0.6 10.0 %copy-start = (s32[2,256]{1,0:T(2,128)S(1)}, s32[2,256]{1,0:T(2,128)}, u32[]{:S(2)}) copy-start(s32[2,256]{1,0:T(2,128)} %ids_ref.3) | copy-start | bytes 6148
  9.0 1.7 %collective-permute-start = (f32[256,256]{1,0:T(8,128)S(1)}, f32[256,256]{1,0:T(8,128)S(1)}, u32[]{:S(2)}, u32[]{:S(2)}) collective-permute-start(f32[256,256]{1,0:T(8,128)S(1)} %get-tuple-element.9), channel_id=1, source_target_pairs={{0,1},{1,0},{2,3},{3,2},{4,5},{5,4},{6,7},{7,6},{8,9},{9,8},{10,11... | collective-permute-start | bytes 786440 | tf_op jit(solution)/shard_map/ppermute | solution.py:220
